TPU v7x, 512 devices: a whole 4x8x8 slice. The times are simulated.
512 devices in a mesh: dp: 16 (over z_lo, x), ctx: 32 (over y, z_hi, core).
Axes of the slice: x: 4, y: 8, z: 8 (z_hi: 2, z_lo: 4; z = z_hi * 4 + z_lo), core: 2. Of those that a mesh axis runs over, the one named last changes fastest.
Arguments:
- queries: bfloat16 [16, 4096, 512], P('dp', 'ctx'), may hold values from -6 to 6
- key_states: bfloat16 [16, 4096, 512], P('dp', 'ctx'), may hold values from -6 to 6
- value_states: bfloat16 [16, 4096, 512], P('dp', 'ctx'), may hold values from -6 to 6
- gate_states: bfloat16 [16, 4096, 512], P('dp', 'ctx'), may hold values from -6 to 6
- out_grad: bfloat16 [16, 4096, 512], P('dp', 'ctx'), may hold values from -6 to 6
- segment_ids: int32 [16, 4096], P('dp'), may hold values from 0 to 3, never falling along the last dimension, each value on 1 to 2048 neighbouring positions
- norm_gain: float32 [512], replicated, may hold values from 0.1 to 1.9
Outputs:
- layer_out: bfloat16 [16, 4096, 512], P('dp', 'ctx')
- query_grad: bfloat16 [16, 4096, 512], P('dp', 'ctx')
- key_grad: bfloat16 [16, 4096, 512], P('dp', 'ctx')
- value_grad: bfloat16 [16, 4096, 512], P('dp', 'ctx')
- gate_grad: bfloat16 [16, 4096, 512], P('dp', 'ctx')
- gain_grad: float32 [512], replicated
Inputs may be any that keep to these rules, and one draw needn't show every extreme that they name: `segment_ids`: in each sample the history numbers never fall, each of the 4 histories has 1 to 2048 positions and one has exactly 2048.
All inputs are finite; a program needn't handle non-finite values.
Results may differ from a plain program's by a relative error of at most 0.0058.
Values may be sent and summed in bfloat16 or wider, within the bound.
No kernel may reach another device: no remote copies, remote signals or barrier semaphores. Data moves between devices by JAX's collectives and lax.ppermute only.
A program may use at most 64 MiB of HBM per device.

v0:
```python
import math
import jax
import jax.numpy as jnp
from jax import lax
from jax.sharding import PartitionSpec as P

HEADS = 4
HSIZE = 128


def head_dot(left_rows, right_rows):
    left_heads = left_rows.reshape(left_rows.shape[0], HEADS, HSIZE)
    right_heads = right_rows.reshape(right_rows.shape[0], HEADS, HSIZE)
    return jnp.einsum("qhd,khd->hqk", left_heads, right_heads, preferred_element_type=jnp.float32)


def head_product(weights, rows):
    rows_heads = rows.reshape(rows.shape[0], HEADS, HSIZE)
    result = jnp.einsum("hqk,khd->qhd", weights, rows_heads, preferred_element_type=jnp.float32)
    return result.reshape(result.shape[0], HEADS * HSIZE)


def head_product_back(weights, rows):
    rows_heads = rows.reshape(rows.shape[0], HEADS, HSIZE)
    result = jnp.einsum("hqk,qhd->khd", weights, rows_heads, preferred_element_type=jnp.float32)
    return result.reshape(result.shape[0], HEADS * HSIZE)


def visible_pairs(query_seg, key_seg):
    return (query_seg[:, None] == key_seg[None, :])[None]


def silu_slope(scores):
    sigmoid = jax.nn.sigmoid(scores)
    return sigmoid * (1.0 + scores * (1.0 - sigmoid))


def per_device(queries, key_states, value_states, gate_states, out_grad, segment_ids, norm_gain):
    scale = HSIZE ** (-0.5)
    tok_rows = queries.shape[1]
    hidden = queries.shape[2]
    seq_len = segment_ids.shape[1]
    segs = segment_ids[0]
    my_first = lax.axis_index("ctx") * tok_rows
    own_seg = lax.dynamic_slice_in_dim(segs, my_first, tok_rows, 0)
    own_query = queries[0]
    own_key = key_states[0]
    own_value = value_states[0]
    all_keys, all_values = (
        lax.all_gather(key_states, "ctx", axis=1, tiled=True),
        lax.all_gather(value_states, "ctx", axis=1, tiled=True),
    )
    all_keys = all_keys[0]
    all_values = all_values[0]
    block = math.gcd(seq_len, 512)
    blocks_count = seq_len // block

    def forward_step(block_id, running):
        key_first = block_id * block
        key_block = lax.dynamic_slice_in_dim(all_keys, key_first, block, 0)
        value_block = lax.dynamic_slice_in_dim(all_values, key_first, block, 0)
        key_seg = lax.dynamic_slice_in_dim(segs, key_first, block, 0)
        scores = scale * head_dot(own_query, key_block)
        visible = visible_pairs(own_seg, key_seg)
        weights = jnp.where(visible, jax.nn.silu(scores), 0.0).astype(jnp.bfloat16)
        return running + head_product(weights, value_block)

    attended = lax.fori_loop(
        0, blocks_count, forward_step, jnp.zeros((tok_rows, hidden), jnp.float32)
    )
    inv_rms = lax.rsqrt(jnp.mean(attended * attended, axis=1, keepdims=True) + 1e-06)
    normed = attended * inv_rms
    gain_row = norm_gain[None, :]
    gate_f = gate_states[0].astype(jnp.float32)
    grad_f = out_grad[0].astype(jnp.float32)
    layer_out = (normed * gain_row * gate_f).astype(jnp.bfloat16)
    gate_grad = (grad_f * normed * gain_row).astype(jnp.bfloat16)
    gain_part = jnp.sum(grad_f * normed * gate_f, axis=0)
    total_rows = lax.axis_size("dp") * lax.axis_size("ctx") * tok_rows
    gain_grad = lax.psum(gain_part, ("dp", "ctx")) / math.sqrt(total_rows)
    normed_grad = grad_f * gain_row * gate_f
    attn_grad = (
        inv_rms * (normed_grad - normed * jnp.mean(normed * normed_grad, axis=1, keepdims=True))
    ).astype(jnp.bfloat16)

    def query_step(block_id, running):
        key_first = block_id * block
        key_block = lax.dynamic_slice_in_dim(all_keys, key_first, block, 0)
        value_block = lax.dynamic_slice_in_dim(all_values, key_first, block, 0)
        key_seg = lax.dynamic_slice_in_dim(segs, key_first, block, 0)
        scores = scale * head_dot(own_query, key_block)
        visible = visible_pairs(own_seg, key_seg)
        value_dot = head_dot(attn_grad, value_block)
        slopes = jnp.where(visible, scale * value_dot * silu_slope(scores), 0.0).astype(
            jnp.bfloat16
        )
        return running + head_product(slopes, key_block)

    query_grad = lax.fori_loop(
        0, blocks_count, query_step, jnp.zeros((tok_rows, hidden), jnp.float32)
    )
    zeros_block = jnp.zeros((tok_rows, hidden), jnp.float32)
    grad_piece = attn_grad[None]
    query_rows = lax.all_gather(queries, "ctx", axis=1, tiled=True)[0]
    grad_rows = lax.all_gather(grad_piece, "ctx", axis=1, tiled=True)[0]
    row_count = grad_rows.shape[0]
    step_rows = math.gcd(row_count, 512)

    def key_step(block_id, totals):
        row_first = block_id * step_rows
        query_block = lax.dynamic_slice_in_dim(query_rows, row_first, step_rows, 0)
        grad_block = lax.dynamic_slice_in_dim(grad_rows, row_first, step_rows, 0)
        query_seg = lax.dynamic_slice_in_dim(segs, row_first, step_rows, 0)
        scores = scale * head_dot(query_block, own_key)
        visible = visible_pairs(query_seg, own_seg)
        weights = jnp.where(visible, jax.nn.silu(scores), 0.0).astype(jnp.bfloat16)
        value_dot = head_dot(grad_block, own_value)
        slopes = jnp.where(visible, scale * value_dot * silu_slope(scores), 0.0).astype(
            jnp.bfloat16
        )
        return (
            totals[0] + head_product_back(slopes, query_block),
            totals[1] + head_product_back(weights, grad_block),
        )

    key_grad, value_grad = lax.fori_loop(
        0, row_count // step_rows, key_step, (zeros_block, zeros_block)
    )
    return (
        layer_out[None],
        query_grad.astype(jnp.bfloat16)[None],
        key_grad.astype(jnp.bfloat16)[None],
        value_grad.astype(jnp.bfloat16)[None],
        gate_grad[None],
        gain_grad,
    )


def solution(mesh):
    return jax.shard_map(
        per_device,
        mesh=mesh,
        in_specs=(
            P("dp", "ctx", None),
            P("dp", "ctx", None),
            P("dp", "ctx", None),
            P("dp", "ctx", None),
            P("dp", "ctx", None),
            P("dp", None),
            P(),
        ),
        out_specs=(
            P("dp", "ctx", None),
            P("dp", "ctx", None),
            P("dp", "ctx", None),
            P("dp", "ctx", None),
            P("dp", "ctx", None),
            P(),
        ),
        check_vma=False,
    )
```

profile of v0, /device:TPU:1, one launch (start us, length us, event | category | flops | bytes accessed | tf_op | source)
XLA Modules:
  0.0 511.9 jit_solution(14382006248976778904)
XLA Ops:
  7.2 1.7 copy.34
  9.7 1.7 copy.38
  13.4 1.6 reshape_squeeze.36
  15.6 111.8 %all-gather.8.cloned.1.call-done = bf16[1,4096,512]{1,2,0:T(8,128)(2,1)} async-done(((bf16[1,128,512]{1,2,0:T(8,128)(2,1)}), bf16[1,4096,512]{1,2,0:T(8,128)(2,1)}) %all-gather.8.cloned.1.call-update) | async-done | bytes 4194320 | tf_op jit(solution)/shard_map/all_gather | solution.py:50
  127.4 104.0 %all-gather.6.cloned.1.call-done = bf16[1,4096,512]{2,1,0:T(8,128)(2,1)} async-done(((bf16[1,128,512]{2,1,0:T(8,128)(2,1)}), bf16[1,4096,512]{2,1,0:T(8,128)(2,1)}) %all-gather.6.cloned.1.call-update) | async-done | bytes 4194320 | tf_op jit(solution)/shard_map/all_gather | solution.py:51
  231.4 32.6 %while.47 = (s32[]{:T(128)}, f32[128,512]{0,1:T(8,128)S(1)}, bf16[4096,512]{1,0:T(8,128)(2,1)}, s32[128]{0:T(128)S(1)}, s32[4096]{0:T(1024)}, /*index=5*/bf16[40...) while((s32[]{:T(128)}, f32[128,512]{0,1:T(8,128)S(1)}, ...), condition=%wide.wide.region_1.2_spmd.clone, body=%wide.wide.region_0.1_spmd.clone.sunk | while | flops 136249344 | bytes 5511865 | solution.py:68
  232.4 1.1 constant_dynamic-slice_fusion.15
  233.7 1.1 constant_dynamic-slice_fusion.16
  236.4 1.1 constant_dynamic-slice_fusion.15
  237.7 1.1 constant_dynamic-slice_fusion.16
  240.5 1.1 constant_dynamic-slice_fusion.15
  241.8 1.1 constant_dynamic-slice_fusion.16
  244.6 1.1 constant_dynamic-slice_fusion.15
  245.9 1.1 constant_dynamic-slice_fusion.16
  248.6 1.1 constant_dynamic-slice_fusion.15
  249.9 1.1 constant_dynamic-slice_fusion.16
  252.7 1.1 constant_dynamic-slice_fusion.15
  254.0 1.1 constant_dynamic-slice_fusion.16
  256.8 1.1 constant_dynamic-slice_fusion.15
  258.1 1.1 constant_dynamic-slice_fusion.16
  260.8 1.1 constant_dynamic-slice_fusion.15
  262.1 1.1 constant_dynamic-slice_fusion.16
  265.9 41.7 %while.48 = (s32[]{:T(128)}, f32[128,512]{0,1:T(8,128)S(1)}, bf16[4096,512]{0,1:T(8,128)(2,1)}, s32[128]{0:T(128)S(1)}, s32[4096]{0:T(1024)}, /*index=5*/bf16[40...) while((s32[]{:T(128)}, f32[128,512]{0,1:T(8,128)S(1)}, ...), condition=%wide.wide.region_5.6_spmd.clone, body=%wide.wide.region_4.5_spmd.clone.sunk | while | flops 204668928 | bytes 6429377 | solution.py:99
  266.0 1.1 constant_dynamic-slice_fusion.17
  269.4 1.7 fusion.118
  271.2 1.1 constant_dynamic-slice_fusion.17
  274.6 1.7 fusion.118
  276.4 1.1 constant_dynamic-slice_fusion.17
  279.8 1.7 fusion.118
  281.6 1.2 constant_dynamic-slice_fusion.17
  285.1 1.7 fusion.118
  286.9 1.1 constant_dynamic-slice_fusion.17
  290.3 1.7 fusion.118
  292.1 1.1 constant_dynamic-slice_fusion.17
  295.5 1.7 fusion.118
  297.3 1.1 constant_dynamic-slice_fusion.17
  300.7 1.7 fusion.118
  302.5 1.1 constant_dynamic-slice_fusion.17
  305.9 1.7 fusion.118
  308.5 101.4 %psum.7 = f32[512]{0:T(512)S(1)} all-reduce(f32[512]{0:T(512)S(1)} %get-tuple-element.541), channel_id=1, replica_groups=mesh['dp'=16,'ctx'=32] {'dp','ctx'}, use_global_device_ids=true, to_apply=%region_9.10 | all-reduce | flops 512 | bytes 4096 | tf_op jit(solution)/shard_map/psum | solution.py:80
  410.4 32.7 %all-gather.12.cloned.1.call-done = bf16[4096,512]{1,0:T(8,128)(2,1)} async-done(((bf16[128,512]{1,0:T(8,128)(2,1)}), bf16[4096,512]{1,0:T(8,128)(2,1)}) %all-gather.12.cloned.1.call-update) | async-done | bytes 4194320 | tf_op jit(solution)/shard_map/all_gather | solution.py:105
  443.1 60.7 %while.49 = (s32[]{:T(128)}, f32[128,512]{0,1:T(8,128)S(1)}, f32[128,512]{0,1:T(8,128)S(1)}, bf16[4096,512]{0,1:T(8,128)(2,1)}, s32[4096]{0:T(1024)}, /*index=5*...) while((s32[]{:T(128)}, f32[128,512]{0,1:T(8,128)S(1)}, ...), condition=%wide.wide.region_7.8_spmd.clone, body=%wide.wide.region_6.7_spmd.clone.sunk | while | flops 273481728 | bytes 11475685 | solution.py:126
  444.2 1.3 convolution_multiply_fusion.7
  448.5 1.6 fusion.126
  450.7 1.1 constant_dynamic-slice_fusion.19
  451.8 1.3 convolution_multiply_fusion.7
  456.0 1.6 fusion.126
  458.3 1.1 constant_dynamic-slice_fusion.19
  459.4 1.3 convolution_multiply_fusion.7
  463.6 1.6 fusion.126
  465.9 1.1 constant_dynamic-slice_fusion.19
  467.0 1.3 convolution_multiply_fusion.7
  471.2 1.6 fusion.126
  473.5 1.1 constant_dynamic-slice_fusion.19
  474.6 1.3 convolution_multiply_fusion.7
  478.8 1.6 fusion.126
  481.1 1.1 constant_dynamic-slice_fusion.19
  482.2 1.3 convolution_multiply_fusion.7
  486.4 1.6 fusion.126
  488.7 1.1 constant_dynamic-slice_fusion.19
  489.8 1.3 convolution_multiply_fusion.7
  494.0 1.6 fusion.126
  497.3 1.3 convolution_multiply_fusion.7
  501.6 1.6 fusion.126
  (188 shorter events, 72.3 us)
Async XLA Ops:
  7.2 120.3 %all-gather.8.cloned.1.call-start = ((), (), s32[]{:S(2)}) async-start(), calls=%async_computation.1 | async-start | bytes 4325376 | tf_op jit(solution)/shard_map/all_gather | solution.py:50
  8.9 222.5 %all-gather.6.cloned.1.call-start = ((), (), s32[]{:S(2)}) async-start(), calls=%async_computation | async-start | bytes 4325376 | tf_op jit(solution)/shard_map/all_gather | solution.py:51
  9.7 400.7 %all-gather.10.cloned.1.call-start = ((), (), s32[]{:S(2)}) async-start(), calls=%async_computation.2 | async-start | bytes 4325376 | tf_op jit(solution)/shard_map/all_gather | solution.py:104
  11.4 431.7 %all-gather.12.cloned.1.call-start = ((), (), s32[]{:S(2)}) async-start(), calls=%async_computation.3 | async-start | bytes 4325376 | tf_op jit(solution)/shard_map/all_gather | solution.py:105
  231.4 32.8 %copy-start.2 = (bf16[1,128,512]{2,1,0:T(8,128)(2,1)S(1)}, bf16[1,128,512]{2,1,0:T(8,128)(2,1)}, u32[]{:S(2)}) copy-start(bf16[1,128,512]{2,1,0:T(8,128)(2,1)} %param.17) | copy-start | bytes 393220
  231.4 32.8 %copy-start.3 = (bf16[1,128,512]{2,1,0:T(8,128)(2,1)S(1)}, bf16[1,128,512]{2,1,0:T(8,128)(2,1)}, u32[]{:S(2)}) copy-start(bf16[1,128,512]{2,1,0:T(8,128)(2,1)} %param.16) | copy-start | bytes 393220
  231.4 32.8 %copy-start.4 = (f32[512]{0:T(512)S(1)}, f32[512]{0:T(512)}, u32[]{:S(2)}) copy-start(f32[512]{0:T(512)} %param.19) | copy-start | bytes 6148
  265.9 177.2 %copy-start = (bf16[1,128,512]{2,1,0:T(8,128)(2,1)S(1)}, bf16[1,128,512]{2,1,0:T(8,128)(2,1)}, u32[]{:S(2)}) copy-start(bf16[1,128,512]{2,1,0:T(8,128)(2,1)} %param.15) | copy-start | bytes 393220
  448.3 1.7 copy-start.1
  455.9 1.7 copy-start.1
  463.5 1.7 copy-start.1
  471.1 1.7 copy-start.1
  478.7 1.7 copy-start.1
  486.3 1.7 copy-start.1
  493.8 1.7 copy-start.1
  501.4 1.7 copy-start.1
Sparse Core Ops, SparseCore 0:
  11.7 115.6 all-gather.7
  130.8 100.6 all-gather.5
  235.1 103.4 all-gather.9
  342.4 100.7 all-gather.11
where the time goes:
time: 516 us; the launch traced here: 512 us
  waiting for transfers between devices  249 us (48%)
  blocking collectives  101 us (20%)
  local copies, waits for them, and re-layouts  84.2 us (16%)
  matrix products  48.8 us (9%)
  between operations  13.9 us (3%)
  other arithmetic  12.6 us (2%)
    all_gather x1, waiting for transfers between devices, per_device(): lax.all_gather(key_states, 'ctx', axis=1, tiled=True)  112 us
    all_gather x1, waiting for transfers between devices, per_device(): lax.all_gather(value_states, 'ctx', axis=1, tiled=True)  104 us
    psum x1, blocking collectives, per_device(): gain_grad = lax.psum(gain_part, ('dp', 'ctx')) / math.sqrt(total_rows)  101 us
    all_gather x1, waiting for transfers between devices, per_device(): grad_rows = lax.all_gather(grad_piece, 'ctx', axis=1, tiled=True)[0]  32.7 us
    dot_general x16, matrix products, head_product(): jnp.einsum('hqk,khd->qhd', weights, rows_heads, preferred_element_type=jn...  19.3 us
    dot_general x16, matrix products, head_product_back(): jnp.einsum('hqk,qhd->khd', weights, rows_heads, preferred_element_type=jn...  16.7 us
    dot_general x16, matrix products, head_dot(): jnp.einsum('qhd,khd->hqk', left_heads, right_heads, preferred_element_typ...  12.8 us
    dynamic_slice x16, local copies, waits for them, and re-layouts, forward_step(): value_block = lax.dynamic_slice_in_dim(all_values, key_first, block, 0)  10.4 us
  transfers between devices with their start and end apart: 4, of which 3 were waited for; matrix products, arithmetic and copies ran while one was open for 16% of the time, Pallas kernels for 0%

commit v1 on v0

--- a/solution.py
+++ b/solution.py
@@ -6,6 +6,11 @@
 
 HEADS = 4
 HSIZE = 128
+
+
+def summed_here(block, axis):
+    blocks = lax.all_gather(block, axis)
+    return jnp.sum(blocks, axis=0)
 
 
 def head_dot(left_rows, right_rows):
@@ -77,7 +82,7 @@
     gate_grad = (grad_f * normed * gain_row).astype(jnp.bfloat16)
     gain_part = jnp.sum(grad_f * normed * gate_f, axis=0)
     total_rows = lax.axis_size("dp") * lax.axis_size("ctx") * tok_rows
-    gain_grad = lax.psum(gain_part, ("dp", "ctx")) / math.sqrt(total_rows)
+    gain_grad = summed_here(gain_part, ("dp", "ctx")) / math.sqrt(total_rows)
     normed_grad = grad_f * gain_row * gate_f
     attn_grad = (
         inv_rms * (normed_grad - normed * jnp.mean(normed * normed_grad, axis=1, keepdims=True))

time: 516 us -> 1260 us (2.44)
  waiting for transfers between devices: 249 us -> 1130 us
  blocking collectives: 101 us -> 0 us
  local copies, waits for them, and re-layouts: 84.2 us -> 68.9 us
  matrix products: 48.8 us -> 34.3 us
    all_gather x0 -> x1, waiting for transfers between devices: none -> 699 us  [summed_here(): blocks = lax.all_gather(block, axis)]
    all_gather x1, waiting for transfers between devices: 0.01 us -> 106 us  [per_device(): query_rows = lax.all_gather(queries, 'ctx', axis=1, tiled=True)[0]]
    psum x1 -> x0, blocking collectives: 101 us -> none  [per_device(): gain_grad = lax.psum(gain_part, ('dp', 'ctx')) / math.sqrt(total_rows)]
    all_gather x1, waiting for transfers between devices: 32.7 us -> 104 us  [per_device(): grad_rows = lax.all_gather(grad_piece, 'ctx', axis=1, tiled=True)[0]]
  transfers between devices with their start and end apart: 4 -> 5, of which waited for: 3 -> 5; matrix products, arithmetic and copies ran while one was open for 16% -> 4% of each run, Pallas kernels for 0% -> 0%
where the time goes in v1:
time: 1260 us
  waiting for transfers between devices  1130 us (90%)
  local copies, waits for them, and re-layouts  68.9 us (5%)
  matrix products  34.3 us (3%)
  between operations  13.9 us (1%)
    all_gather x1, waiting for transfers between devices, summed_here(): blocks = lax.all_gather(block, axis)  699 us
    all_gather x1, waiting for transfers between devices, per_device(): lax.all_gather(value_states, 'ctx', axis=1, tiled=True)  115 us
    all_gather x1, waiting for transfers between devices, per_device(): lax.all_gather(key_states, 'ctx', axis=1, tiled=True)  107 us
    all_gather x1, waiting for transfers between devices, per_device(): query_rows = lax.all_gather(queries, 'ctx', axis=1, tiled=True)[0]  106 us
    all_gather x1, waiting for transfers between devices, per_device(): grad_rows = lax.all_gather(grad_piece, 'ctx', axis=1, tiled=True)[0]  104 us
  transfers between devices with their start and end apart: 5, of which 5 were waited for; matrix products, arithmetic and copies ran while one was open for 4% of the time, Pallas kernels for 0%

profile of v1, /device:TPU:1, one launch (start us, length us, event | category | flops | bytes accessed | tf_op | source)
XLA Modules:
  0.0 1260.0 jit_solution(10519574359270290174)
XLA Ops:
  7.2 1.7 copy.72
  9.0 1.7 copy.73
  10.7 0.9 reshape_squeeze.32
  12.3 115.1 %all-gather.9.cloned.1.call-done = bf16[1,4096,512]{1,2,0:T(8,128)(2,1)} async-done(((bf16[1,128,512]{1,2,0:T(8,128)(2,1)}), bf16[1,4096,512]{1,2,0:T(8,128)(2,1)}) %all-gather.9.cloned.1.call-update) | async-done | bytes 4194320 | tf_op jit(solution)/shard_map/all_gather | solution.py:56
  127.4 106.9 %all-gather.11.cloned.1.call-done = bf16[1,4096,512]{1,2,0:T(8,128)(2,1)} async-done(((bf16[1,128,512]{1,2,0:T(8,128)(2,1)}), bf16[1,4096,512]{1,2,0:T(8,128)(2,1)}) %all-gather.11.cloned.1.call-update) | async-done | bytes 4194320 | tf_op jit(solution)/shard_map/all_gather | solution.py:55
  234.3 23.7 %while.47 = (s32[]{:T(128)}, f32[128,512]{0,1:T(8,128)S(1)}, bf16[4096,512]{0,1:T(8,128)(2,1)}, s32[128]{0:T(128)S(1)}, s32[4096]{0:T(1024)}, /*index=5*/bf16[40...) while((s32[]{:T(128)}, f32[128,512]{0,1:T(8,128)S(1)}, ...), condition=%wide.wide.region_1.2_spmd.clone, body=%wide.wide.region_0.1_spmd.clone.sunk | while | flops 136249344 | bytes 4463285 | solution.py:73
  234.4 1.3 constant_dynamic-slice_fusion.14
  235.7 0.8 dynamic_slice.101
  237.4 1.3 constant_dynamic-slice_fusion.14
  238.7 0.8 dynamic_slice.101
  240.3 1.3 constant_dynamic-slice_fusion.14
  241.6 0.8 dynamic_slice.101
  243.3 1.3 constant_dynamic-slice_fusion.14
  244.6 0.8 dynamic_slice.101
  246.3 1.3 constant_dynamic-slice_fusion.14
  247.5 0.8 dynamic_slice.101
  249.2 1.3 constant_dynamic-slice_fusion.14
  250.5 0.8 dynamic_slice.101
  252.2 1.3 constant_dynamic-slice_fusion.14
  253.5 0.8 dynamic_slice.101
  255.1 1.3 constant_dynamic-slice_fusion.14
  256.4 0.8 dynamic_slice.101
  258.3 1.5 fusion.59
  259.9 1.7 copy.76
  261.6 0.9 reshape_squeeze.34
  263.3 0.8 multiply_convert_fusion.1
  264.1 34.4 %while.48 = (s32[]{:T(128)}, f32[128,512]{0,1:T(8,128)S(1)}, bf16[4096,512]{0,1:T(8,128)(2,1)}, s32[128]{0:T(128)S(1)}, s32[4096]{0:T(1024)}, /*index=5*/bf16[40...) while((s32[]{:T(128)}, f32[128,512]{0,1:T(8,128)S(1)}, ...), condition=%wide.wide.region_5.6_spmd.clone, body=%wide.wide.region_4.5_spmd.clone.sunk | while | flops 204668928 | bytes 7215805 | solution.py:104
  264.2 1.3 constant_dynamic-slice_fusion.15
  266.7 1.7 fusion.123
  268.5 1.3 constant_dynamic-slice_fusion.15
  271.0 1.7 fusion.123
  272.8 1.3 constant_dynamic-slice_fusion.15
  275.3 1.7 fusion.123
  277.1 1.3 constant_dynamic-slice_fusion.15
  279.6 1.7 fusion.123
  281.4 1.3 constant_dynamic-slice_fusion.15
  283.9 1.7 fusion.123
  285.7 1.3 constant_dynamic-slice_fusion.15
  288.2 1.7 fusion.123
  290.0 1.3 constant_dynamic-slice_fusion.15
  292.5 1.7 fusion.123
  294.3 1.3 constant_dynamic-slice_fusion.15
  296.8 1.7 fusion.123
  299.3 698.6 %all-gather.17.cloned.1.call-done = f32[512,1,512]{2,1,0:T(1,128)} async-done(((f32[1,1,512]{2,1,0:T(1,128)}), f32[512,1,512]{2,1,0:T(1,128)}) %all-gather.17.cloned.1.call-update) | async-done | bytes 1048592 | tf_op jit(solution)/shard_map/all_gather | solution.py:12
  997.9 1.8 reduce_sum.39
  1000.3 106.2 %all-gather.13.cloned.1.call-done = bf16[1,4096,512]{1,2,0:T(8,128)(2,1)} async-done(((bf16[1,128,512]{1,2,0:T(8,128)(2,1)}), bf16[1,4096,512]{1,2,0:T(8,128)(2,1)}) %all-gather.13.cloned.1.call-update) | async-done | bytes 4194320 | tf_op jit(solution)/shard_map/all_gather | solution.py:109
  1106.5 104.4 %all-gather.15.cloned.1.call-done = bf16[4096,512]{1,0:T(8,128)(2,1)} async-done(((bf16[128,512]{1,0:T(8,128)(2,1)}), bf16[4096,512]{1,0:T(8,128)(2,1)}) %all-gather.15.cloned.1.call-update) | async-done | bytes 4194320 | tf_op jit(solution)/shard_map/all_gather | solution.py:110
  1210.9 41.0 %while.49 = (s32[]{:T(128)}, f32[128,512]{0,1:T(8,128)S(1)}, f32[128,512]{0,1:T(8,128)S(1)}, bf16[4096,512]{0,1:T(8,128)(2,1)}, s32[4096]{0:T(1024)}, /*index=5*...) while((s32[]{:T(128)}, f32[128,512]{0,1:T(8,128)S(1)}, ...), condition=%wide.wide.region_7.8_spmd.clone, body=%wide.wide.region_6.7_spmd.clone.sunk | while | flops 273481728 | bytes 11475693 | solution.py:131
  1210.9 1.1 constant_dynamic-slice_fusion.17
  1213.3 1.1 constant_dynamic-slice_fusion.16
  1216.0 1.1 constant_dynamic-slice_fusion.17
  1218.4 1.1 constant_dynamic-slice_fusion.16
  1221.2 1.1 constant_dynamic-slice_fusion.17
  1223.5 1.1 constant_dynamic-slice_fusion.16
  1226.3 1.1 constant_dynamic-slice_fusion.17
  1228.7 1.1 constant_dynamic-slice_fusion.16
  1231.4 1.1 constant_dynamic-slice_fusion.17
  1233.8 1.1 constant_dynamic-slice_fusion.16
  1236.5 1.1 constant_dynamic-slice_fusion.17
  1238.9 1.1 constant_dynamic-slice_fusion.16
  1241.7 1.1 constant_dynamic-slice_fusion.17
  1244.1 1.1 constant_dynamic-slice_fusion.16
  1246.8 1.1 constant_dynamic-slice_fusion.17
  1249.2 1.1 constant_dynamic-slice_fusion.16
  (163 shorter events, 44.9 us)
Async XLA Ops:
  7.2 120.3 %all-gather.9.cloned.1.call-start = ((), (), s32[]{:S(2)}) async-start(), calls=%async_computation | async-start | bytes 4325376 | tf_op jit(solution)/shard_map/all_gather | solution.py:56
  8.9 225.4 %all-gather.11.cloned.1.call-start = ((), (), s32[]{:S(2)}) async-start(), calls=%async_computation.1 | async-start | bytes 4325376 | tf_op jit(solution)/shard_map/all_gather | solution.py:55
  10.6 987.2 %all-gather.17.cloned.1.call-start = ((), (), s32[]{:S(2)}) async-start(), calls=%async_computation.4 | async-start | bytes 1050624 | tf_op jit(solution)/shard_map/all_gather | solution.py:12
  234.3 24.0 %copy-start = (bf16[1,128,512]{2,1,0:T(8,128)(2,1)S(1)}, bf16[1,128,512]{2,1,0:T(8,128)(2,1)}, u32[]{:S(2)}) copy-start(bf16[1,128,512]{2,1,0:T(8,128)(2,1)} %param.17) | copy-start | bytes 393220
  234.3 24.0 %copy-start.1 = (bf16[1,128,512]{2,1,0:T(8,128)(2,1)S(1)}, bf16[1,128,512]{2,1,0:T(8,128)(2,1)}, u32[]{:S(2)}) copy-start(bf16[1,128,512]{2,1,0:T(8,128)(2,1)} %param.16) | copy-start | bytes 393220
  234.3 24.0 %copy-start.5 = (f32[512]{0:T(512)S(1)}, f32[512]{0:T(512)}, u32[]{:S(2)}) copy-start(f32[512]{0:T(512)} %param.19) | copy-start | bytes 6148
  234.3 28.3 %copy-start.3 = (bf16[1,128,512]{2,1,0:T(8,128)(2,1)S(1)}, bf16[1,128,512]{2,1,0:T(8,128)(2,1)}, u32[]{:S(2)}) copy-start(bf16[1,128,512]{2,1,0:T(8,128)(2,1)} %param.14) | copy-start | bytes 393220
  234.3 28.3 %copy-start.2 = (bf16[1,128,512]{2,1,0:T(8,128)(2,1)S(1)}, bf16[1,128,512]{2,1,0:T(8,128)(2,1)}, u32[]{:S(2)}) copy-start(bf16[1,128,512]{2,1,0:T(8,128)(2,1)} %param.15) | copy-start | bytes 393220
  259.8 846.7 %all-gather.13.cloned.1.call-start = ((), (), s32[]{:S(2)}) async-start(), calls=%async_computation.2 | async-start | bytes 4325376 | tf_op jit(solution)/shard_map/all_gather | solution.py:109
  261.6 949.3 %all-gather.15.cloned.1.call-start = ((), (), s32[]{:S(2)}) async-start(), calls=%async_computation.3 | async-start | bytes 4325376 | tf_op jit(solution)/shard_map/all_gather | solution.py:110
  1210.9 3.7 copy-start.4
  1216.0 3.7 copy-start.4
  1221.1 3.7 copy-start.4
  1226.3 3.7 copy-start.4
  1231.4 3.7 copy-start.4
  1236.5 3.7 copy-start.4
  1241.7 3.7 copy-start.4
  1246.8 3.7 copy-start.4
Sparse Core Ops, SparseCore 0:
  11.7 115.6 all-gather.8
  131.1 103.1 all-gather.10
  259.9 737.9 all-gather.16
  1001.5 104.9 all-gather.12
  1110.2 100.6 all-gather.14
